TPU v7x, 32 devices: a whole 2x2x4 slice. The times are simulated.
32 devices in a mesh: groups: 2 (over y), dp: 4 (over z), tensor: 4 (over x, core).
Axes of the slice: x: 2, y: 2, z: 4, core: 2. Of those that a mesh axis runs over, the one named last changes fastest.
Arguments:
- activations: bfloat16 [2048, 16384], P(('groups', 'dp'), 'tensor'), parts along dimension 0, may hold values from -6 to 6
- out_grads: bfloat16 [2048, 8192], P(('groups', 'dp'), 'tensor'), parts along dimension 0, may hold values from -6 to 6
- eigen_in: bfloat16 [32, 512, 512], P('tensor'), may hold values from -0.25 to 0.25
- eigen_out: bfloat16 [16, 512, 512], P('tensor'), may hold values from -0.25 to 0.25
- feature_order: int32 [4, 4096], P('tensor'), may hold values from 0 to 4095, each once within a row
- query_left: bfloat16 [32, 4, 8192], P('dp', None, 'tensor'), may hold values from -0.0625 to 0.0625
- query_right: bfloat16 [32, 4, 16384], P('dp', None, 'tensor'), may hold values from -0.046875 to 0.046875
- owner_plan: int32 [4], replicated, may hold values from 0 to 3, each once
- example_slot: int32 [2048], P(('groups', 'dp')), parts along dimension 0, may hold values from 0 to 15
Outputs:
- scores: float32 [128, 32], P(('groups', 'dp'), 'tensor'), parts along dimension 0
There are 2 independent parts, one for each index of `groups`. A program takes and returns all parts, laid end to end along the dimension named above; an argument that names none is the same for every part. Nothing has to cross between parts.
All inputs are finite; a program needn't handle non-finite values.
Results may differ from a plain program's by a relative error of at most 0.004.
Values may be sent and summed in bfloat16 or wider, within the bound.
A program may use at most 64 MiB of HBM per device.

v0:
```python
import jax
import jax.numpy as jnp
from jax import lax
from jax.sharding import PartitionSpec as P

EX_DEV = 16


def spread(block, axis, holder):
    block = jnp.where(lax.axis_index(axis) == holder, block, jnp.zeros_like(block))
    return lax.psum(block, axis)


def project(rotated, factor_rows):
    return lax.dot_general(
        rotated, factor_rows, (((1,), (1,)), ((), ())), preferred_element_type=jnp.float32
    )


def rotate_blocks(values, blocks):
    row_count = values.shape[0]
    block_width = blocks.shape[1]
    shaped = values.reshape(row_count, blocks.shape[0], block_width)
    turned = jnp.einsum("tbi,bij->tbj", shaped, blocks, preferred_element_type=jnp.float32)
    return turned.astype(jnp.bfloat16).reshape(row_count, values.shape[1])


def local(
    activations,
    out_grads,
    eigen_in,
    eigen_out,
    feature_order,
    query_left,
    query_right,
    owner_plan,
    example_slot,
):
    row_count = activations.shape[0]
    factor_rank = query_left.shape[1]
    ordered_acts = jnp.take(activations, feature_order[0], axis=1)
    rotated_acts = rotate_blocks(ordered_acts, eigen_in)
    rotated_grads = rotate_blocks(out_grads, eigen_out)
    left_rows = query_left.reshape(-1, query_left.shape[2])
    right_rows = query_right.reshape(-1, query_right.shape[2])
    panel_width = left_rows.shape[0]
    dp_count = lax.axis_size("dp")
    empty = jnp.zeros((row_count, dp_count * panel_width), jnp.float32)

    def one_round(round_index, stores):
        owner_index = owner_plan[round_index]
        panel_left, panel_right = (
            spread(left_rows, "dp", owner_index),
            spread(right_rows, "dp", owner_index),
        )
        left_part = project(rotated_grads, panel_left)
        right_part = project(rotated_acts, panel_right)
        column = round_index * panel_width
        return (
            lax.dynamic_update_slice_in_dim(stores[0], left_part, column, 1),
            lax.dynamic_update_slice_in_dim(stores[1], right_part, column, 1),
        )

    left_store, right_store = lax.fori_loop(0, dp_count, one_round, (empty, empty))
    share_width = left_store.shape[1] // lax.axis_size("tensor")
    left_total, right_total = lax.psum((left_store, right_store), "tensor")
    offset = lax.axis_index("tensor") * share_width
    left_mine = lax.dynamic_slice_in_dim(left_total, offset, share_width, 1)
    right_mine = lax.dynamic_slice_in_dim(right_total, offset, share_width, 1)
    token_scores = (
        (left_mine * right_mine)
        .reshape(row_count, share_width // factor_rank, factor_rank)
        .sum(axis=2)
    )
    one_hot = (example_slot[None, :] == jnp.arange(EX_DEV, dtype=jnp.int32)[:, None]).astype(
        jnp.float32
    )
    return jnp.dot(one_hot, token_scores, precision=lax.Precision.HIGHEST)


def solution(mesh):
    placed = (
        P(("groups", "dp"), "tensor"),
        P(("groups", "dp"), "tensor"),
        P("tensor", None, None),
        P("tensor", None, None),
        P("tensor", None),
        P("dp", None, "tensor"),
        P("dp", None, "tensor"),
        P(),
        P(("groups", "dp")),
    )
    return jax.shard_map(
        local, mesh=mesh, in_specs=placed, out_specs=P(("groups", "dp"), "tensor"), check_vma=False
    )
```

profile of v0, /device:TPU:0, one launch (start us, length us, event | category | flops | bytes accessed | tf_op | source)
XLA Modules:
  0.0 276.4 jit_solution(17612158975224186180)
XLA Ops:
  7.4 4.2 %copy.24 = bf16[256,4096]{0,1:T(8,128)(2,1)} copy(bf16[256,4096]{1,0:T(8,128)(2,1)} %param.11) | data formatting | bytes 4194304 | tf_op args[0]
  11.6 17.7 %gather_fusion = bf16[4096,256]{1,0:T(8,128)(2,1)} fusion(bf16[256,4096]{0,1:T(8,128)(2,1)} %copy.24, s32[4096]{0:T(1024)S(1)} %broadcast_clamp_fusion), kind=kCustom, calls=%fused_computation | custom fusion | bytes 4210688 | tf_op jit(solution)/shard_map/jit(_take)/gather | solution.py:41
  29.4 3.9 %copy.25 = bf16[256,8,512]{2,0,1:T(8,128)(2,1)} copy(bf16[256,8,512]{0,2,1:T(8,128)(2,1)} %bitcast.49) | data formatting | bytes 4194304 | tf_op jit(solution)/shard_map/jit(_take)/gather | solution.py:41
  34.4 5.4 %convert_bitcast_fusion = bf16[256,8,512]{2,0,1:T(8,128)(2,1)} fusion(bf16[8,512,512]{2,1,0:T(8,128)(2,1)} %param.13, bf16[256,8,512]{2,0,1:T(8,128)(2,1)} %copy.25, pred[8,512]{1,0:T(8,128)(4,1)S(1)} %compare_and_fusion), kind=kOutput, calls=%fused_computation.7 | convolution fusion | flops 1075838976 | bytes 8392704 | tf_op jit(solution)/shard_map/tbi,bij->tbj/dot_general | solution.py:24
  39.8 3.9 %copy.26 = bf16[256,8,512]{0,2,1:T(8,128)(2,1)} copy(bf16[256,8,512]{2,0,1:T(8,128)(2,1)} %convert_bitcast_fusion) | data formatting | bytes 4194304 | tf_op jit(solution)/shard_map/convert_element_type | solution.py:25
  43.7 4.2 %copy.28 = bf16[256,4096]{1,0:T(8,128)(2,1)} copy(bf16[256,4096]{0,1:T(8,128)(2,1)} %bitcast.48) | data formatting | bytes 4194304 | tf_op jit(solution)/shard_map/while | solution.py:64
  47.8 1.9 convolution_convert_fusion
  49.7 1.5 copy.27
  51.2 1.0 reshape.63
  52.3 0.9 reshape.60
  53.2 0.7 broadcast_in_dim.15
  53.9 0.7 broadcast_in_dim.15.clone
  54.5 178.9 %while.15 = (s32[]{:T(128)}, f32[256,128]{0,1:T(8,128)}, f32[256,128]{0,1:T(8,128)}, s32[4]{0:T(128)S(1)}, bf16[32,2048]{1,0:T(8,128)(2,1)S(1)}, /*index=5*/bf16...) while((s32[]{:T(128)}, f32[256,128]{0,1:T(8,128)}, ...), condition=%wide.region_3.4_spmd, body=%wide.region_0.3_spmd.sunk | while | flops 101056520 | bytes 7274806 | solution.py:64
  55.7 0.7 broadcast_select_fusion.5
  57.1 40.6 %all-reduce.9.cloned.1.call-done = (bf16[32,2048]{1,0:T(8,128)(2,1)}, bf16[32,4096]{1,0:T(8,128)(2,1)}) async-done(((bf16[32,2048]{1,0:T(8,128)(2,1)}, bf16[32,4096]{1,0:T(8,128)(2,1)}), (bf16[32,2048]{1,0:T(8,128)(2,1)}, bf16[32,4096]{1,0:T(8,128)(2,1)})) %all-reduce.9.cloned.1.call-update) | async-done | bytes 393232 | tf_op jit(solution)/shard_map/while/body/eval_jaxpr/psum | solution.py:11
  97.7 3.1 %fusion.31 = f32[256,128]{0,1:T(8,128)} fusion(f32[256,128]{0,1:T(8,128)} %get-tuple-element.260, s32[]{:T(128)S(6)} %select_n.96, bf16[32,4096]{1,0:T(8,128)(2,1)} %get-tuple-element.243, bf16[256,4096]{1,0:T(8,128)(2,1)} %get-tuple-element.279), kind=kOutput, calls=%fused_computation.4.clone.1 | convolution fusion | flops 67108864 | bytes 2392068 | tf_op jit(solution)/shard_map/while/body/eval_jaxpr/dot_general | solution.py:15
  100.7 1.0 fusion.30
  102.9 0.7 broadcast_select_fusion.5
  104.3 37.4 %all-reduce.9.cloned.1.call-done = (bf16[32,2048]{1,0:T(8,128)(2,1)}, bf16[32,4096]{1,0:T(8,128)(2,1)}) async-done(((bf16[32,2048]{1,0:T(8,128)(2,1)}, bf16[32,4096]{1,0:T(8,128)(2,1)}), (bf16[32,2048]{1,0:T(8,128)(2,1)}, bf16[32,4096]{1,0:T(8,128)(2,1)})) %all-reduce.9.cloned.1.call-update) | async-done | bytes 393232 | tf_op jit(solution)/shard_map/while/body/eval_jaxpr/psum | solution.py:11
  141.7 3.1 %fusion.31 = f32[256,128]{0,1:T(8,128)} fusion(f32[256,128]{0,1:T(8,128)} %get-tuple-element.260, s32[]{:T(128)S(6)} %select_n.96, bf16[32,4096]{1,0:T(8,128)(2,1)} %get-tuple-element.243, bf16[256,4096]{1,0:T(8,128)(2,1)} %get-tuple-element.279), kind=kOutput, calls=%fused_computation.4.clone.1 | convolution fusion | flops 67108864 | bytes 2392068 | tf_op jit(solution)/shard_map/while/body/eval_jaxpr/dot_general | solution.py:15
  144.7 1.0 fusion.30
  146.9 0.7 broadcast_select_fusion.5
  148.3 37.4 %all-reduce.9.cloned.1.call-done = (bf16[32,2048]{1,0:T(8,128)(2,1)}, bf16[32,4096]{1,0:T(8,128)(2,1)}) async-done(((bf16[32,2048]{1,0:T(8,128)(2,1)}, bf16[32,4096]{1,0:T(8,128)(2,1)}), (bf16[32,2048]{1,0:T(8,128)(2,1)}, bf16[32,4096]{1,0:T(8,128)(2,1)})) %all-reduce.9.cloned.1.call-update) | async-done | bytes 393232 | tf_op jit(solution)/shard_map/while/body/eval_jaxpr/psum | solution.py:11
  185.7 3.1 %fusion.31 = f32[256,128]{0,1:T(8,128)} fusion(f32[256,128]{0,1:T(8,128)} %get-tuple-element.260, s32[]{:T(128)S(6)} %select_n.96, bf16[32,4096]{1,0:T(8,128)(2,1)} %get-tuple-element.243, bf16[256,4096]{1,0:T(8,128)(2,1)} %get-tuple-element.279), kind=kOutput, calls=%fused_computation.4.clone.1 | convolution fusion | flops 67108864 | bytes 2392068 | tf_op jit(solution)/shard_map/while/body/eval_jaxpr/dot_general | solution.py:15
  188.7 1.0 fusion.30
  190.9 0.7 broadcast_select_fusion.5
  192.3 37.0 %all-reduce.9.cloned.1.call-done = (bf16[32,2048]{1,0:T(8,128)(2,1)}, bf16[32,4096]{1,0:T(8,128)(2,1)}) async-done(((bf16[32,2048]{1,0:T(8,128)(2,1)}, bf16[32,4096]{1,0:T(8,128)(2,1)}), (bf16[32,2048]{1,0:T(8,128)(2,1)}, bf16[32,4096]{1,0:T(8,128)(2,1)})) %all-reduce.9.cloned.1.call-update) | async-done | bytes 393232 | tf_op jit(solution)/shard_map/while/body/eval_jaxpr/psum | solution.py:11
  229.4 3.1 %fusion.31 = f32[256,128]{0,1:T(8,128)} fusion(f32[256,128]{0,1:T(8,128)} %get-tuple-element.260, s32[]{:T(128)S(6)} %select_n.96, bf16[32,4096]{1,0:T(8,128)(2,1)} %get-tuple-element.243, bf16[256,4096]{1,0:T(8,128)(2,1)} %get-tuple-element.279), kind=kOutput, calls=%fused_computation.4.clone.1 | convolution fusion | flops 67108864 | bytes 2392068 | tf_op jit(solution)/shard_map/while/body/eval_jaxpr/dot_general | solution.py:15
  232.4 1.0 fusion.30
  234.0 33.7 %all-reduce.7.cloned.1.call-done = (f32[256,128]{0,1:T(8,128)}, f32[256,128]{0,1:T(8,128)}) async-done(((f32[256,128]{0,1:T(8,128)}, f32[256,128]{0,1:T(8,128)}), (f32[256,128]{0,1:T(8,128)}, f32[256,128]{0,1:T(8,128)})) %all-reduce.7.cloned.1.call-update) | async-done | bytes 262160 | tf_op jit(solution)/shard_map/psum | solution.py:66
  267.7 0.8 dynamic-slice_multiply_fusion
  268.6 0.7 fusion.10
  (44 shorter events, 6.8 us)
Async XLA Ops:
  7.4 40.5 %copy-start = (bf16[4,512,512]{2,1,0:T(8,128)(2,1)S(1)}, bf16[4,512,512]{2,1,0:T(8,128)(2,1)}, u32[]{:S(2)}) copy-start(bf16[4,512,512]{2,1,0:T(8,128)(2,1)} %param.14) | copy-start | bytes 6291460
  7.4 4.2 %copy-start.2 = (s32[1,4096]{1,0:T(1,128)S(1)}, s32[1,4096]{1,0:T(1,128)}, u32[]{:S(2)}) copy-start(s32[1,4096]{1,0:T(1,128)} %param.15) | copy-start | bytes 49156
  43.7 4.2 %copy-start.4 = (bf16[256,2048]{1,0:T(8,128)(2,1)S(1)}, bf16[256,2048]{1,0:T(8,128)(2,1)}, u32[]{:S(2)}) copy-start(bf16[256,2048]{1,0:T(8,128)(2,1)} %param.12) | copy-start | bytes 3145732
  49.7 4.8 %copy-start.5 = (s32[4]{0:T(128)S(1)}, s32[4]{0:T(128)}, u32[]{:S(2)}) copy-start(s32[4]{0:T(128)} %param.18) | copy-start | bytes 52
  54.5 214.0 %copy-start.3 = (s32[256]{0:T(256)S(1)}, s32[256]{0:T(256)}, u32[]{:S(2)}) copy-start(s32[256]{0:T(256)} %param.19) | copy-start | bytes 3076
  54.5 43.1 %all-reduce.9.cloned.1.call-start = ((), (), s32[]{:S(2)}) async-start(), calls=%async_computation.1 | async-start | bytes 786432 | tf_op jit(solution)/shard_map/while/body/eval_jaxpr/psum | solution.py:11
  97.7 3.1 %copy-start.1 = (bf16[32,2048]{1,0:T(8,128)(2,1)S(1)}, bf16[32,2048]{1,0:T(8,128)(2,1)}, u32[]{:S(2)}) copy-start(bf16[32,2048]{1,0:T(8,128)(2,1)} %get-tuple-element.242) | copy-start | bytes 393220 | tf_op jit(solution)/shard_map/while
  101.7 39.9 %all-reduce.9.cloned.1.call-start = ((), (), s32[]{:S(2)}) async-start(), calls=%async_computation.1 | async-start | bytes 786432 | tf_op jit(solution)/shard_map/while/body/eval_jaxpr/psum | solution.py:11
  141.7 3.1 %copy-start.1 = (bf16[32,2048]{1,0:T(8,128)(2,1)S(1)}, bf16[32,2048]{1,0:T(8,128)(2,1)}, u32[]{:S(2)}) copy-start(bf16[32,2048]{1,0:T(8,128)(2,1)} %get-tuple-element.242) | copy-start | bytes 393220 | tf_op jit(solution)/shard_map/while
  145.7 39.9 %all-reduce.9.cloned.1.call-start = ((), (), s32[]{:S(2)}) async-start(), calls=%async_computation.1 | async-start | bytes 786432 | tf_op jit(solution)/shard_map/while/body/eval_jaxpr/psum | solution.py:11
  185.7 3.1 %copy-start.1 = (bf16[32,2048]{1,0:T(8,128)(2,1)S(1)}, bf16[32,2048]{1,0:T(8,128)(2,1)}, u32[]{:S(2)}) copy-start(bf16[32,2048]{1,0:T(8,128)(2,1)} %get-tuple-element.242) | copy-start | bytes 393220 | tf_op jit(solution)/shard_map/while
  189.8 39.6 %all-reduce.9.cloned.1.call-start = ((), (), s32[]{:S(2)}) async-start(), calls=%async_computation.1 | async-start | bytes 786432 | tf_op jit(solution)/shard_map/while/body/eval_jaxpr/psum | solution.py:11
  229.4 3.1 %copy-start.1 = (bf16[32,2048]{1,0:T(8,128)(2,1)S(1)}, bf16[32,2048]{1,0:T(8,128)(2,1)}, u32[]{:S(2)}) copy-start(bf16[32,2048]{1,0:T(8,128)(2,1)} %get-tuple-element.242) | copy-start | bytes 393220 | tf_op jit(solution)/shard_map/while
  233.4 34.3 %all-reduce.7.cloned.1.call-start = ((), (), s32[]{:S(2)}) async-start(), calls=%async_computation | async-start | bytes 524288 | tf_op jit(solution)/shard_map/psum | solution.py:66
Sparse Core Ops, SparseCore 0:
  57.9 39.7 all-reduce.8
  105.1 36.4 all-reduce.8
  149.1 36.4 all-reduce.8
  192.8 36.4 all-reduce.8
Sparse Core Ops, SparseCore 1:
  236.3 31.4 all-reduce.6
where the time goes:
time: 277 us; the launch traced here: 276 us
  waiting for transfers between devices  187 us (68%)
  local copies, waits for them, and re-layouts  41.5 us (15%)
  matrix products  24.3 us (9%)
  between operations  14.6 us (5%)
  other arithmetic  6.92 us (2%)
    psum x4, waiting for transfers between devices, spread(): return lax.psum(block, axis)  152 us
    psum x1, waiting for transfers between devices, local(): left_total, right_total = lax.psum((left_store, right_store), 'tensor')  33.7 us
    gather x2, local copies, waits for them, and re-layouts, local(): ordered_acts = jnp.take(activations, feature_order[0], axis=1)  21.6 us
    dot_general x8, matrix products, project(): lax.dot_general(rotated, factor_rows, (((1,), (1,)), ((), ())), preferred...  16.3 us
    dot_general x2, matrix products, rotate_blocks(): jnp.einsum('tbi,bij->tbj', shaped, blocks, preferred_element_type=jnp.flo...  7.27 us
    while x2, local copies, waits for them, and re-layouts, local(): lax.fori_loop(0, dp_count, one_round, (empty, empty))  5.65 us
  transfers between devices with their start and end apart: 5, of which 5 were waited for; matrix products, arithmetic and copies ran while one was open for 0% of the time, Pallas kernels for 0%

commit v1 on v0

v1 whole, which is shorter than its diff:
```python
import functools

import jax
import jax.numpy as jnp
from jax import lax
from jax.experimental import pallas as pl
from jax.experimental.pallas import tpu as pltpu
from jax.sharding import PartitionSpec as P

EX_DEV = 16
MESH = pl.DeviceIdType.MESH
NT = (((1,), (1,)), ((), ()))


def kernel(
    dims,
    plan_ref,
    order_ref,
    slot_ref,
    acts_hbm,
    grads_hbm,
    ein_hbm,
    eout_hbm,
    query_hbm,
    out_ref,
    acts,
    grads,
    ein,
    eout,
    panels,
    rot,
    parts,
    send_buf,
    recv_buf,
    load_sem,
    zsend_sem,
    zrecv_sem,
    ysend_sem,
    yrecv_sem,
    tsend_sem,
    trecv_sem,
):
    dp, tensor, groups, chunks = dims
    y = lax.axis_index("groups")
    z = lax.axis_index("dp")
    x = lax.axis_index("tensor")
    other = groups - 1 - y
    panel_rows = panels.shape[1]
    half = panel_rows // groups
    width = panels.shape[2] // chunks
    left_width = grads.shape[1]
    right_width = acts.shape[1]
    blk = ein.shape[1]
    share = dp // tensor

    loads = [
        pltpu.make_async_copy(query_hbm, panels.at[z], load_sem.at[0]),
        pltpu.make_async_copy(grads_hbm, grads, load_sem.at[1]),
        pltpu.make_async_copy(eout_hbm, eout, load_sem.at[2]),
        pltpu.make_async_copy(acts_hbm, acts, load_sem.at[3]),
        pltpu.make_async_copy(ein_hbm, ein, load_sem.at[4]),
    ]
    for load in loads:
        load.start()

    barrier = pltpu.get_barrier_semaphore()
    has_up = z + 1 < dp
    has_down = z > 0

    @pl.when(has_up)
    def _():
        pl.semaphore_signal(barrier, inc=1, device_id={"dp": z + 1}, device_id_type=MESH)

    @pl.when(has_down)
    def _():
        pl.semaphore_signal(barrier, inc=1, device_id={"dp": z - 1}, device_id_type=MESH)

    pl.semaphore_signal(barrier, inc=1, device_id={"groups": other}, device_id_type=MESH)
    for hop in range(1, tensor):
        pl.semaphore_signal(
            barrier, inc=1, device_id={"tensor": lax.rem(x + hop, tensor)}, device_id_type=MESH
        )
    edge = jnp.where(has_up, 1, 0) + jnp.where(has_down, 1, 0)
    pl.semaphore_wait(barrier, tensor + edge)

    def piece(panel, group, chunk):
        rows = pl.ds(pl.multiple_of(group * half, half), half)
        return panels.at[panel, rows, pl.ds(chunk * width, width)]

    def z_copy(up, panel, chunk):
        ref = piece(panel, y, chunk)
        return pltpu.make_async_remote_copy(
            src_ref=ref,
            dst_ref=ref,
            send_sem=zsend_sem.at[0 if up else 1, panel, chunk],
            recv_sem=zrecv_sem.at[panel, chunk],
            device_id={"dp": z + 1 if up else z - 1},
            device_id_type=MESH,
        )

    def y_copy(panel, group, chunk):
        ref = piece(panel, group, chunk)
        return pltpu.make_async_remote_copy(
            src_ref=ref,
            dst_ref=ref,
            send_sem=ysend_sem.at[panel, chunk],
            recv_sem=yrecv_sem.at[panel, chunk],
            device_id={"groups": other},
            device_id_type=MESH,
        )

    loads[0].wait()
    for chunk in range(chunks):

        @pl.when(has_up)
        def _():
            z_copy(True, z, chunk).start()

        @pl.when(has_down)
        def _():
            z_copy(False, z, chunk).start()

    def relay(step, chunk):
        for up in (True, False):
            panel = z - step if up else z + step
            valid = panel >= 0 if up else panel < dp
            onward = has_up if up else has_down

            @pl.when(valid)
            def _():
                copy = z_copy(up, panel, chunk)
                copy.wait_recv()

                @pl.when(onward)
                def _():
                    copy.start()

                y_copy(panel, y, chunk).start()

    def rotate_left(block):
        cols = slice(block * blk, (block + 1) * blk)
        turned = jnp.dot(grads[:, cols], eout[block], preferred_element_type=jnp.float32)
        rot[:, cols] = turned.astype(jnp.bfloat16)

    def rotate_right(block):
        cols = slice(block * blk, (block + 1) * blk)
        wanted = order_ref[:, cols]
        depth = min(1024, right_width)
        total = None
        for base in range(0, right_width, depth):
            index = lax.broadcasted_iota(jnp.int32, (depth, blk), 0) + base
            picks = jnp.where(index == wanted, 1.0, 0.0).astype(jnp.bfloat16)
            term = jnp.dot(
                acts[:, base : base + depth], picks, preferred_element_type=jnp.float32
            )
            total = term if total is None else total + term
        ordered = total.astype(jnp.bfloat16)
        turned = jnp.dot(ordered, ein[block], preferred_element_type=jnp.float32)
        rot[:, left_width + block * blk : left_width + (block + 1) * blk] = turned.astype(
            jnp.bfloat16
        )

    relays = [(step, chunk) for step in range(1, dp) for chunk in range(chunks)]
    work = [(rotate_left, block) for block in range(eout.shape[0])]
    work += [(rotate_right, block) for block in range(ein.shape[0])]
    done = 0
    for index, (job, block) in enumerate(work):
        if index == 0:
            loads[1].wait()
            loads[2].wait()
        if index == eout.shape[0]:
            loads[3].wait()
            loads[4].wait()
        job(block)
        until = (index + 1) * len(relays) // len(work)
        for step, chunk in relays[done:until]:
            relay(step, chunk)
        done = until

    def each_foreign(body):
        for step in range(1, dp):
            for up in (True, False):
                panel = z - step if up else z + step
                valid = panel >= 0 if up else panel < dp

                @pl.when(valid)
                def _():
                    for chunk in range(chunks):
                        body(up, panel, chunk)

    each_foreign(lambda up, panel, chunk: y_copy(panel, other, chunk).wait_recv())

    for panel in range(dp):
        parts[0, panel] = lax.dot_general(
            panels[panel, :, :left_width], rot[:, :left_width], NT, preferred_element_type=jnp.float32
        )
        parts[1, panel] = lax.dot_general(
            panels[panel, :, left_width:], rot[:, left_width:], NT, preferred_element_type=jnp.float32
        )

    def gather_share(hop):
        target = lax.rem(x + hop, tensor)
        for place in range(share):
            owner = plan_ref[target * share + place]
            for side in range(2):
                total = jnp.zeros_like(parts[side, 0])
                for panel in range(dp):
                    total = jnp.where(owner == panel, parts[side, panel], total)
                send_buf[hop, side, place * panel_rows : (place + 1) * panel_rows] = total

    def t_copy(hop):
        return pltpu.make_async_remote_copy(
            src_ref=send_buf.at[hop],
            dst_ref=recv_buf.at[hop],
            send_sem=tsend_sem.at[hop],
            recv_sem=trecv_sem.at[hop],
            device_id={"tensor": lax.rem(x + hop, tensor)},
            device_id_type=MESH,
        )

    for hop in range(1, tensor):
        gather_share(hop)
        t_copy(hop).start()
    gather_share(0)
    left = send_buf[0, 0]
    right = send_buf[0, 1]

    @pl.when(has_up)
    def _():
        for chunk in range(chunks):
            z_copy(True, z, chunk).wait_send()

    @pl.when(has_down)
    def _():
        for chunk in range(chunks):
            z_copy(False, z, chunk).wait_send()

    def drain(up, panel, chunk):
        y_copy(panel, y, chunk).wait_send()

        @pl.when(has_up if up else has_down)
        def _():
            z_copy(up, panel, chunk).wait_send()

    each_foreign(drain)

    for hop in range(1, tensor):
        t_copy(hop).wait()
        left += recv_buf[hop, 0]
        right += recv_buf[hop, 1]
    product = left * right
    examples = lax.broadcasted_iota(jnp.int32, (EX_DEV, slot_ref.shape[1]), 0)
    one_hot = jnp.where(examples == slot_ref[...], 1.0, 0.0).astype(jnp.float32)
    sums = lax.dot_general(
        one_hot, product, NT, precision=lax.Precision.HIGHEST, preferred_element_type=jnp.float32
    )
    queries = out_ref.shape[1]
    rank = sums.shape[1] // queries
    row = lax.broadcasted_iota(jnp.int32, (sums.shape[1], queries), 0)
    col = lax.broadcasted_iota(jnp.int32, (sums.shape[1], queries), 1)
    fold = jnp.where((row >= col * rank) & (row < (col + 1) * rank), 1.0, 0.0).astype(jnp.float32)
    out_ref[...] = jnp.dot(
        sums, fold, precision=lax.Precision.HIGHEST, preferred_element_type=jnp.float32
    )


def local(
    activations,
    out_grads,
    eigen_in,
    eigen_out,
    feature_order,
    query_left,
    query_right,
    owner_plan,
    example_slot,
):
    dp = lax.axis_size("dp")
    tensor = lax.axis_size("tensor")
    groups = lax.axis_size("groups")
    tokens, right_width = activations.shape
    left_width = out_grads.shape[1]
    panel_rows = query_left.shape[0] * query_left.shape[1]
    width = left_width + right_width
    query = jnp.concatenate([query_left, query_right], axis=2).reshape(panel_rows, width)
    chunks = 3
    share = dp // tensor
    bf16, f32 = jnp.bfloat16, jnp.float32
    vmem = pl.BlockSpec(memory_space=pltpu.VMEM)
    anywhere = pl.BlockSpec(memory_space=pl.ANY)
    dma = pltpu.SemaphoreType.DMA
    return pl.pallas_call(
        functools.partial(kernel, (dp, tensor, groups, chunks)),
        out_shape=jax.ShapeDtypeStruct((EX_DEV, share * query_left.shape[0]), f32),
        in_specs=[pl.BlockSpec(memory_space=pltpu.SMEM), vmem, vmem] + [anywhere] * 5,
        out_specs=vmem,
        scratch_shapes=[
            pltpu.VMEM(activations.shape, bf16),
            pltpu.VMEM(out_grads.shape, bf16),
            pltpu.VMEM(eigen_in.shape, bf16),
            pltpu.VMEM(eigen_out.shape, bf16),
            pltpu.VMEM((dp, panel_rows, width), bf16),
            pltpu.VMEM((tokens, width), bf16),
            pltpu.VMEM((2, dp, panel_rows, tokens), f32),
            pltpu.VMEM((tensor, 2, share * panel_rows, tokens), f32),
            pltpu.VMEM((tensor, 2, share * panel_rows, tokens), f32),
            dma((5,)),
            dma((2, dp, chunks)),
            dma((dp, chunks)),
            dma((dp, chunks)),
            dma((dp, chunks)),
            dma((tensor,)),
            dma((tensor,)),
        ],
        compiler_params=pltpu.CompilerParams(
            collective_id=0, has_side_effects=True, vmem_limit_bytes=56 * 1024 * 1024
        ),
    )(
        owner_plan,
        feature_order,
        example_slot[None, :],
        activations,
        out_grads,
        eigen_in,
        eigen_out,
        query,
    )


def solution(mesh):
    placed = (
        P(("groups", "dp"), "tensor"),
        P(("groups", "dp"), "tensor"),
        P("tensor", None, None),
        P("tensor", None, None),
        P("tensor", None),
        P("dp", None, "tensor"),
        P("dp", None, "tensor"),
        P(),
        P(("groups", "dp")),
    )
    return jax.shard_map(
        local, mesh=mesh, in_specs=placed, out_specs=P(("groups", "dp"), "tensor"), check_vma=False
    )
```

time: 277 us -> 39.5 us (0.14)
  waiting for transfers between devices: 187 us -> 0 us
  local copies, waits for them, and re-layouts: 41.5 us -> 2.18 us
  Pallas kernels: 0 us -> 35.8 us
  matrix products: 24.3 us -> 0 us
  between operations: 14.6 us -> 0.01 us
  other arithmetic: 6.92 us -> 1.16 us
    psum x5 -> x0, waiting for transfers between devices: 186 us -> none  [the longest x4 152 us: spread(): return lax.psum(block, axis)]
    pallas_call x0 -> x1, Pallas kernels: none -> 35.8 us  [local(): pl.pallas_call(functools.partial(kernel, (dp, tensor, groups, chunks)), o...]
    dot_general x11 -> x0, matrix products: 24.3 us -> none  [the longest x8 16.3 us: project(): lax.dot_general(rotated, factor_rows, (((1,), (1,)), ((), ())), preferred...]
    gather x2 -> x0, local copies, waits for them, and re-layouts: 21.6 us -> none  [local(): ordered_acts = jnp.take(activations, feature_order[0], axis=1)]
    while x10 -> x0, local copies, waits for them, and re-layouts: 5.67 us -> none  [the longest x2 5.65 us: local(): lax.fori_loop(0, dp_count, one_round, (empty, empty))]
    select_n x9 -> x0, other arithmetic: 5.51 us -> none  [the longest x8 5.49 us: spread(): jnp.where(lax.axis_index(axis) == holder, block, jnp.zeros_like(block))]
    unnamed x12 -> x0, local copies, waits for them, and re-layouts: 4.75 us -> none
    convert_element_type x1 -> x0, local copies, waits for them, and re-layouts: 3.89 us -> none  [rotate_blocks(): return turned.astype(jnp.bfloat16).reshape(row_count, values.shape[1])]
  transfers between devices with their start and end apart: 5 -> 0, of which waited for: 5 -> 0; matrix products, arithmetic and copies ran while one was open for 0% -> 0% of each run, Pallas kernels for 0% -> 0%
where the time goes in v1:
time: 39.5 us; the launch traced here: 39.2 us
  Pallas kernels  35.8 us (91%)
  local copies, waits for them, and re-layouts  2.18 us (6%)
  other arithmetic  1.16 us (3%)
    pallas_call x1, Pallas kernels, local(): pl.pallas_call(functools.partial(kernel, (dp, tensor, groups, chunks)), o...  35.8 us
    pallas_call x1, local copies, waits for them, and re-layouts, local(): pl.pallas_call(functools.partial(kernel, (dp, tensor, groups, chunks)), o...  1.36 us
    concatenate x1, other arithmetic, local(): jnp.concatenate([query_left, query_right], axis=2)  1.16 us
    reshape x1, local copies, waits for them, and re-layouts, local(): jnp.concatenate([query_left, query_right], axis=2)  0.83 us

profile of v1, /device:TPU:0, one launch (start us, length us, event | category | flops | bytes accessed | tf_op | source)
XLA Modules:
  0.0 39.2 jit_solution(18437109798544292685)
XLA Ops:
  0.0 1.2 %pad_maximum_fusion = bf16[8,4,6144]{2,1,0:T(4,128)(2,1)S(1)} fusion(bf16[8,4,4096]{2,1,0:T(4,128)(2,1)} %param.15, bf16[8,4,2048]{2,1,0:T(4,128)(2,1)} %param.14), kind=kLoop, calls=%fused_computation | loop fusion | flops 786432 | bytes 786432 | tf_op jit(solution)/shard_map/concatenate | solution.py:285
  1.2 0.8 %reshape.3.query_hbm = bf16[32,6144]{1,0:T(8,128)(2,1)} reshape(bf16[8,4,6144]{2,1,0:T(4,128)(2,1)S(1)} %pad_maximum_fusion) | data formatting | bytes 786432 | tf_op jit(solution)/shard_map/reshape | solution.py:285
  2.0 35.8 %shard_map.91 = f32[16,8]{1,0:T(8,128)} custom-call(s32[4]{0:T(128)} %plan_ref.1, s32[1,4096]{1,0:T(1,128)} %order_ref.1, s32[1,256]{1,0:T(1,128)} %bitcast.1, bf16[256,4096]{1,0:T(8,128)(2,1)} %acts_hbm.1, bf16[256,2048]{1,0:T(8,128)(2,1)} %grads_hbm.1, bf16[8,512,512]{2,1,0:T(8,128)(2,1)} %ein_hbm.1, bf16[4,512,512]{2,1,0:T(8,128)(2,1)} %eout_hbm.1, ...), custom_call_target="tpu_custom_call" | custom-call | tf_op jit(solution)/shard_map/pallas_call | solution.py:292
  37.8 1.4 %copy.10 = f32[16,8]{0,1:T(8,128)} copy(f32[16,8]{1,0:T(8,128)} %shard_map.91) | data formatting | bytes 1024 | tf_op jit(solution)/shard_map/pallas_call | solution.py:292

commit v2 on v1

--- a/solution.py
+++ b/solution.py
@@ -21,12 +21,17 @@
     grads_hbm,
     ein_hbm,
     eout_hbm,
-    query_hbm,
+    ql_hbm,
+    qr_hbm,
     out_ref,
     acts,
     grads,
     ein,
     eout,
+    ql_stage,
+    qr_stage,
+    wide,
+    ordered,
     panels,
     rot,
     parts,
@@ -54,11 +59,12 @@
     share = dp // tensor
 
     loads = [
-        pltpu.make_async_copy(query_hbm, panels.at[z], load_sem.at[0]),
-        pltpu.make_async_copy(grads_hbm, grads, load_sem.at[1]),
-        pltpu.make_async_copy(eout_hbm, eout, load_sem.at[2]),
-        pltpu.make_async_copy(acts_hbm, acts, load_sem.at[3]),
-        pltpu.make_async_copy(ein_hbm, ein, load_sem.at[4]),
+        pltpu.make_async_copy(ql_hbm, ql_stage, load_sem.at[0]),
+        pltpu.make_async_copy(qr_hbm, qr_stage, load_sem.at[1]),
+        pltpu.make_async_copy(grads_hbm, grads, load_sem.at[2]),
+        pltpu.make_async_copy(eout_hbm, eout, load_sem.at[3]),
+        pltpu.make_async_copy(acts_hbm, acts, load_sem.at[4]),
+        pltpu.make_async_copy(ein_hbm, ein, load_sem.at[5]),
     ]
     for load in loads:
         load.start()
@@ -80,9 +86,6 @@
         pl.semaphore_signal(
             barrier, inc=1, device_id={"tensor": lax.rem(x + hop, tensor)}, device_id_type=MESH
         )
-    edge = jnp.where(has_up, 1, 0) + jnp.where(has_down, 1, 0)
-    pl.semaphore_wait(barrier, tensor + edge)
-
     def piece(panel, group, chunk):
         rows = pl.ds(pl.multiple_of(group * half, half), half)
         return panels.at[panel, rows, pl.ds(chunk * width, width)]
@@ -109,9 +112,17 @@
             device_id_type=MESH,
         )
 
-    loads[0].wait()
-    for chunk in range(chunks):
-
+    rank = ql_stage.shape[1]
+
+    def stage(source, base):
+        for query in range(source.shape[0]):
+            wide[query * rank : (query + 1) * rank, base : base + source.shape[2]] = source[
+                query
+            ].astype(jnp.float32)
+        span = slice(base, base + source.shape[2])
+        panels[z, :, span] = wide[:, span].astype(jnp.bfloat16)
+
+    def launch(chunk):
         @pl.when(has_up)
         def _():
             z_copy(True, z, chunk).start()
@@ -119,6 +130,19 @@
         @pl.when(has_down)
         def _():
             z_copy(False, z, chunk).start()
+
+    loads[0].wait()
+    stage(ql_stage, 0)
+    edge = jnp.where(has_up, 1, 0) + jnp.where(has_down, 1, 0)
+    pl.semaphore_wait(barrier, tensor + edge)
+    ahead = 2
+    left_chunks = left_width // width
+    for chunk in range(min(ahead, left_chunks)):
+        launch(chunk)
+    loads[1].wait()
+    stage(qr_stage, left_width)
+    for chunk in range(left_chunks, ahead):
+        launch(chunk)
 
     def relay(step, chunk):
         for up in (True, False):
@@ -142,40 +166,128 @@
         turned = jnp.dot(grads[:, cols], eout[block], preferred_element_type=jnp.float32)
         rot[:, cols] = turned.astype(jnp.bfloat16)
 
-    def rotate_right(block):
-        cols = slice(block * blk, (block + 1) * blk)
+    parts_per_block = 2
+
+    def order_columns(block, part):
+        span = blk // parts_per_block
+        cols = slice(block * blk + part * span, block * blk + (part + 1) * span)
         wanted = order_ref[:, cols]
         depth = min(1024, right_width)
         total = None
         for base in range(0, right_width, depth):
-            index = lax.broadcasted_iota(jnp.int32, (depth, blk), 0) + base
+            index = lax.broadcasted_iota(jnp.int32, (depth, span), 0) + base
             picks = jnp.where(index == wanted, 1.0, 0.0).astype(jnp.bfloat16)
             term = jnp.dot(
                 acts[:, base : base + depth], picks, preferred_element_type=jnp.float32
             )
             total = term if total is None else total + term
-        ordered = total.astype(jnp.bfloat16)
-        turned = jnp.dot(ordered, ein[block], preferred_element_type=jnp.float32)
-        rot[:, left_width + block * blk : left_width + (block + 1) * blk] = turned.astype(
-            jnp.bfloat16
+        ordered[:, part * span : (part + 1) * span] = total.astype(jnp.bfloat16)
+        if part == parts_per_block - 1:
+            turned = jnp.dot(ordered[...], ein[block], preferred_element_type=jnp.float32)
+            start = left_width + block * blk
+            rot[:, start : start + blk] = turned.astype(jnp.bfloat16)
+
+    def arrive(step, chunk):
+        for up in (True, False):
+            panel = z - step if up else z + step
+
+            @pl.when(panel >= 0 if up else panel < dp)
+            def _():
+                y_copy(panel, other, chunk).wait_recv()
+
+    def project(chunk):
+        side = 0 if chunk < left_chunks else 1
+        cols = slice(chunk * width, (chunk + 1) * width)
+        term = lax.dot_general(
+            panels[:, :, cols].reshape(dp * panel_rows, width),
+            rot[:, cols],
+            NT,
+            preferred_element_type=jnp.float32,
+        ).reshape(parts.shape[1:])
+        if chunk in (0, left_chunks):
+            parts[side] = term
+        else:
+            parts[side] += term
+
+    def gather_share(hop, side):
+        target = lax.rem(x + hop, tensor)
+        for place in range(share):
+            owner = plan_ref[target * share + place]
+            total = jnp.zeros_like(parts[side, 0])
+            for panel in range(dp):
+                total = jnp.where(owner == panel, parts[side, panel], total)
+            send_buf[hop, side, place * panel_rows : (place + 1) * panel_rows] = total
+
+    def t_copy(hop, side):
+        return pltpu.make_async_remote_copy(
+            src_ref=send_buf.at[hop, side],
+            dst_ref=recv_buf.at[hop, side],
+            send_sem=tsend_sem.at[hop, side],
+            recv_sem=trecv_sem.at[hop, side],
+            device_id={"tensor": lax.rem(x + hop, tensor)},
+            device_id_type=MESH,
         )
 
-    relays = [(step, chunk) for step in range(1, dp) for chunk in range(chunks)]
-    work = [(rotate_left, block) for block in range(eout.shape[0])]
-    work += [(rotate_right, block) for block in range(ein.shape[0])]
+    def reduce_side(side):
+        for hop in [*range(1, tensor), 0]:
+            gather_share(hop, side)
+            if hop:
+                t_copy(hop, side).start()
+
+    work = [(rotate_left, (block,)) for block in range(eout.shape[0])]
+    work += [
+        (order_columns, (block, part))
+        for block in range(ein.shape[0])
+        for part in range(parts_per_block)
+    ]
+    events = [(chunk, 0, chunk) for chunk in range(ahead, chunks)]
+    events += [
+        (chunk + step * ahead, step, chunk) for step in range(1, dp) for chunk in range(chunks)
+    ]
+    events.sort()
     done = 0
-    for index, (job, block) in enumerate(work):
-        if index == 0:
-            loads[1].wait()
-            loads[2].wait()
-        if index == eout.shape[0]:
-            loads[3].wait()
-            loads[4].wait()
-        job(block)
-        until = (index + 1) * len(relays) // len(work)
-        for step, chunk in relays[done:until]:
+
+    def advance(until):
+        nonlocal done
+        for index, (job, where) in enumerate(work[done:until], done):
+            if index == 0:
+                loads[2].wait()
+                loads[3].wait()
+            if index == eout.shape[0]:
+                loads[4].wait()
+                loads[5].wait()
+            job(*where)
+        done = max(done, until)
+
+    def finish(chunk):
+        if chunk >= left_chunks:
+            last_block = (chunk + 1) * width - left_width
+            advance(eout.shape[0] + parts_per_block * (-(-last_block // blk)))
+        else:
+            advance(eout.shape[0])
+        for step in range(1, dp):
+            arrive(step, chunk)
+        project(chunk)
+        if chunk == left_chunks - 1:
+            reduce_side(0)
+
+    lag = 2
+    ready = []
+    for index, (_, step, chunk) in enumerate(events):
+        if step:
+            advance((index + 1) * len(work) // len(events))
             relay(step, chunk)
-        done = until
+        else:
+            launch(chunk)
+        if step == dp - 1 and chunk < chunks - 1:
+            ready.append((index + lag, chunk))
+        while ready and ready[0][0] <= index:
+            finish(ready.pop(0)[1])
+    for _, chunk in ready:
+        finish(chunk)
+    advance(len(work))
+    finish(chunks - 1)
+    reduce_side(1)
 
     def each_foreign(body):
         for step in range(1, dp):
@@ -188,40 +300,6 @@
                     for chunk in range(chunks):
                         body(up, panel, chunk)
 
-    each_foreign(lambda up, panel, chunk: y_copy(panel, other, chunk).wait_recv())
-
-    for panel in range(dp):
-        parts[0, panel] = lax.dot_general(
-            panels[panel, :, :left_width], rot[:, :left_width], NT, preferred_element_type=jnp.float32
-        )
-        parts[1, panel] = lax.dot_general(
-            panels[panel, :, left_width:], rot[:, left_width:], NT, preferred_element_type=jnp.float32
-        )
-
-    def gather_share(hop):
-        target = lax.rem(x + hop, tensor)
-        for place in range(share):
-            owner = plan_ref[target * share + place]
-            for side in range(2):
-                total = jnp.zeros_like(parts[side, 0])
-                for panel in range(dp):
-                    total = jnp.where(owner == panel, parts[side, panel], total)
-                send_buf[hop, side, place * panel_rows : (place + 1) * panel_rows] = total
-
-    def t_copy(hop):
-        return pltpu.make_async_remote_copy(
-            src_ref=send_buf.at[hop],
-            dst_ref=recv_buf.at[hop],
-            send_sem=tsend_sem.at[hop],
-            recv_sem=trecv_sem.at[hop],
-            device_id={"tensor": lax.rem(x + hop, tensor)},
-            device_id_type=MESH,
-        )
-
-    for hop in range(1, tensor):
-        gather_share(hop)
-        t_copy(hop).start()
-    gather_share(0)
     left = send_buf[0, 0]
     right = send_buf[0, 1]
 
@@ -245,7 +323,8 @@
     each_foreign(drain)
 
     for hop in range(1, tensor):
-        t_copy(hop).wait()
+        for side in range(2):
+            t_copy(hop, side).wait()
         left += recv_buf[hop, 0]
         right += recv_buf[hop, 1]
     product = left * right
@@ -255,7 +334,6 @@
         one_hot, product, NT, precision=lax.Precision.HIGHEST, preferred_element_type=jnp.float32
     )
     queries = out_ref.shape[1]
-    rank = sums.shape[1] // queries
     row = lax.broadcasted_iota(jnp.int32, (sums.shape[1], queries), 0)
     col = lax.broadcasted_iota(jnp.int32, (sums.shape[1], queries), 1)
     fold = jnp.where((row >= col * rank) & (row < (col + 1) * rank), 1.0, 0.0).astype(jnp.float32)
@@ -282,7 +360,6 @@
     left_width = out_grads.shape[1]
     panel_rows = query_left.shape[0] * query_left.shape[1]
     width = left_width + right_width
-    query = jnp.concatenate([query_left, query_right], axis=2).reshape(panel_rows, width)
     chunks = 3
     share = dp // tensor
     bf16, f32 = jnp.bfloat16, jnp.float32
@@ -292,25 +369,29 @@
     return pl.pallas_call(
         functools.partial(kernel, (dp, tensor, groups, chunks)),
         out_shape=jax.ShapeDtypeStruct((EX_DEV, share * query_left.shape[0]), f32),
-        in_specs=[pl.BlockSpec(memory_space=pltpu.SMEM), vmem, vmem] + [anywhere] * 5,
+        in_specs=[pl.BlockSpec(memory_space=pltpu.SMEM), vmem, vmem] + [anywhere] * 6,
         out_specs=vmem,
         scratch_shapes=[
             pltpu.VMEM(activations.shape, bf16),
             pltpu.VMEM(out_grads.shape, bf16),
             pltpu.VMEM(eigen_in.shape, bf16),
             pltpu.VMEM(eigen_out.shape, bf16),
+            pltpu.VMEM(query_left.shape, bf16),
+            pltpu.VMEM(query_right.shape, bf16),
+            pltpu.VMEM((panel_rows, width), f32),
+            pltpu.VMEM((tokens, eigen_in.shape[1]), bf16),
             pltpu.VMEM((dp, panel_rows, width), bf16),
             pltpu.VMEM((tokens, width), bf16),
             pltpu.VMEM((2, dp, panel_rows, tokens), f32),
             pltpu.VMEM((tensor, 2, share * panel_rows, tokens), f32),
             pltpu.VMEM((tensor, 2, share * panel_rows, tokens), f32),
-            dma((5,)),
+            dma((6,)),
             dma((2, dp, chunks)),
             dma((dp, chunks)),
             dma((dp, chunks)),
             dma((dp, chunks)),
-            dma((tensor,)),
-            dma((tensor,)),
+            dma((tensor, 2)),
+            dma((tensor, 2)),
         ],
         compiler_params=pltpu.CompilerParams(
             collective_id=0, has_side_effects=True, vmem_limit_bytes=56 * 1024 * 1024
@@ -323,7 +404,8 @@
         out_grads,
         eigen_in,
         eigen_out,
-        query,
+        query_left,
+        query_right,
     )
 
 

time: 39.5 us -> 31.4 us (0.79)
  Pallas kernels: 35.8 us -> 29.8 us
  other arithmetic: 1.16 us -> 0 us
  local copies, waits for them, and re-layouts: 2.18 us -> 1.36 us
    pallas_call x1, Pallas kernels: 35.8 us -> 29.8 us  [local(): pl.pallas_call(functools.partial(kernel, (dp, tensor, groups, chunks)), o...]
    concatenate x1 -> x0, other arithmetic: 1.16 us -> none  [local(): jnp.concatenate([query_left, query_right], axis=2)]
    reshape x1 -> x0, local copies, waits for them, and re-layouts: 0.83 us -> none  [local(): jnp.concatenate([query_left, query_right], axis=2)]
where the time goes in v2:
time: 31.4 us; the launch traced here: 31.1 us
  Pallas kernels  29.8 us (95%)
  local copies, waits for them, and re-layouts  1.36 us (4%)
    pallas_call x1, Pallas kernels, local(): pl.pallas_call(functools.partial(kernel, (dp, tensor, groups, chunks)), o...  29.8 us
    pallas_call x1, local copies, waits for them, and re-layouts, local(): pl.pallas_call(functools.partial(kernel, (dp, tensor, groups, chunks)), o...  1.36 us

profile of v2, /device:TPU:0, one launch (start us, length us, event | category | flops | bytes accessed | tf_op | source)
XLA Modules:
  0.0 31.1 jit_solution(18123255509316865369)
XLA Ops:
  0.0 29.8 %shard_map.91 = f32[16,8]{1,0:T(8,128)} custom-call(s32[4]{0:T(128)} %plan_ref.1, s32[1,4096]{1,0:T(1,128)} %order_ref.1, s32[1,256]{1,0:T(1,128)} %bitcast.1, bf16[256,4096]{1,0:T(8,128)(2,1)} %acts_hbm.1, bf16[256,2048]{1,0:T(8,128)(2,1)} %grads_hbm.1, bf16[8,512,512]{2,1,0:T(8,128)(2,1)} %ein_hbm.1, bf16[4,512,512]{2,1,0:T(8,128)(2,1)} %eout_hbm.1, ...), custom_call_target="tpu_custom_call" | custom-call | tf_op jit(solution)/shard_map/pallas_call | solution.py:369
  29.8 1.4 %copy.10 = f32[16,8]{0,1:T(8,128)} copy(f32[16,8]{1,0:T(8,128)} %shard_map.91) | data formatting | bytes 1024 | tf_op jit(solution)/shard_map/pallas_call | solution.py:369

commit v3 on v2

--- a/solution.py
+++ b/solution.py
@@ -229,7 +229,7 @@
         )
 
     def reduce_side(side):
-        for hop in [*range(1, tensor), 0]:
+        for hop in [*sorted(range(1, tensor), key=lambda hop: abs(2 * hop - tensor)), 0]:
             gather_share(hop, side)
             if hop:
                 t_copy(hop, side).start()
@@ -271,12 +271,12 @@
         if chunk == left_chunks - 1:
             reduce_side(0)
 
-    lag = 2
+    lag = 3
     ready = []
     for index, (_, step, chunk) in enumerate(events):
         if step:
+            relay(step, chunk)
             advance((index + 1) * len(work) // len(events))
-            relay(step, chunk)
         else:
             launch(chunk)
         if step == dp - 1 and chunk < chunks - 1:

time: 31.4 us -> 31.3 us (level)
  no operation moved by 1% of the time
where the time goes in v3:
time: 31.3 us; the launch traced here: 31.1 us
  Pallas kernels  29.7 us (95%)
  local copies, waits for them, and re-layouts  1.36 us (4%)
    pallas_call x1, Pallas kernels, local(): pl.pallas_call(functools.partial(kernel, (dp, tensor, groups, chunks)), o...  29.7 us
    pallas_call x1, local copies, waits for them, and re-layouts, local(): pl.pallas_call(functools.partial(kernel, (dp, tensor, groups, chunks)), o...  1.36 us

profile of v3, /device:TPU:0, one launch (start us, length us, event | category | flops | bytes accessed | tf_op | source)
XLA Modules:
  0.0 31.1 jit_solution(2995524542744979910)
XLA Ops:
  0.0 29.7 %shard_map.91 = f32[16,8]{1,0:T(8,128)} custom-call(s32[4]{0:T(128)} %plan_ref.1, s32[1,4096]{1,0:T(1,128)} %order_ref.1, s32[1,256]{1,0:T(1,128)} %bitcast.1, bf16[256,4096]{1,0:T(8,128)(2,1)} %acts_hbm.1, bf16[256,2048]{1,0:T(8,128)(2,1)} %grads_hbm.1, bf16[8,512,512]{2,1,0:T(8,128)(2,1)} %ein_hbm.1, bf16[4,512,512]{2,1,0:T(8,128)(2,1)} %eout_hbm.1, ...), custom_call_target="tpu_custom_call" | custom-call | tf_op jit(solution)/shard_map/pallas_call | solution.py:369
  29.7 1.4 %copy.10 = f32[16,8]{0,1:T(8,128)} copy(f32[16,8]{1,0:T(8,128)} %shard_map.91) | data formatting | bytes 1024 | tf_op jit(solution)/shard_map/pallas_call | solution.py:369
